TPU v7x, 512 devices: a whole 4x4x16 slice. The times are simulated.
512 devices in a mesh: section: 2 (over core), context: 32 (over z, y_lo), tensor: 8 (over x, y_hi).
Axes of the slice: x: 4, y: 4 (y_hi: 2, y_lo: 2; y = y_hi * 2 + y_lo), z: 16, core: 2. Of those that a mesh axis runs over, the one named last changes fastest.
Arguments:
- queries: bfloat16 [2, 512, 8192], P('section', 'context', 'tensor'), may hold values from -6 to 6
- turn_keys: bfloat16 [2, 512, 1024], P('section', 'context', 'tensor'), may hold values from -12 to 12
- turn_values: bfloat16 [2, 512, 1024], P('section', 'context', 'tensor'), may hold values from -6 to 6
- cache_keys: bfloat16 [2, 65536, 1024], P('section', 'context', 'tensor'), may hold values from -6 to 6
- cache_values: bfloat16 [2, 65536, 1024], P('section', 'context', 'tensor'), may hold values from -6 to 6
- positions: int32 [2, 512], P('section'), may hold values from 0 to 511, each once within a row
- span_bounds: int32 [2, 4, 2], P('section'), may hold values from 0 to 512, as said below
- residual: bfloat16 [2, 512, 8192], P('section', 'tensor', 'context'), may hold values from -3 to 3
- out_weight: bfloat16 [2, 8192, 8192], P('section', 'tensor', 'context'), may hold values from -0.0625 to 0.0625
Outputs:
- handed: bfloat16 [2, 512, 8192], P('section', 'tensor', 'context')
Inputs may be any that keep to these rules, and one draw needn't show every extreme that they name: `positions`: each row lists every position of the turn once. `span_bounds`: span j lies within positions j * 128 to (j + 1) * 128, is at least 32 positions long; the first span starts at 0 and the last ends at 512.
All inputs are finite; a program needn't handle non-finite values.
Results may differ from a plain program's by a relative error of at most 0.0035.
Values may be sent and summed in bfloat16 or wider, within the bound.
A program may use at most 64 MiB of HBM per device.

v0:
```python
import math

import jax
import jax.numpy as jnp
from jax import lax
from jax.sharding import PartitionSpec as P

HD = 128


NEG = -1e30


def shifted(block, axis, distance):
    devices = range(lax.axis_size(axis))
    route = [((i - distance) % len(devices), i) for i in devices]
    return lax.ppermute(block, axis, route)


def span_mask(own_position, all_position, bounds):
    starts = bounds[:, 0]
    ends = bounds[:, 1]

    def inside(position):
        return (
            (starts[None, :] <= position[:, None]) & (position[:, None] < ends[None, :])
        ).astype(jnp.float32)

    same = (
        jnp.dot(inside(own_position), inside(all_position).T, preferred_element_type=jnp.float32)
        > 0.5
    )
    return (all_position[None, :] <= own_position[:, None]) | same


def partial_attend(query_rows, keys, values, allowed):
    count = query_rows.shape[0]
    kv_count = keys.shape[1] // HD
    head_count = query_rows.shape[1] // HD
    group = head_count // kv_count
    query_split = query_rows.reshape(count, kv_count, group, HD)
    key_split = keys.reshape(keys.shape[0], kv_count, HD)
    value_split = values.reshape(values.shape[0], kv_count, HD)
    scores = jnp.einsum(
        "rgqd,kgd->rgqk", query_split, key_split, preferred_element_type=jnp.float32
    ) * HD ** (-0.5)
    if allowed is not None:
        scores = jnp.where(allowed[:, None, None, :], scores, NEG)
    top = jnp.max(scores, axis=-1)
    expo = jnp.exp(scores - top[..., None])
    total = jnp.sum(expo, axis=-1)
    probs = expo.astype(jnp.bfloat16)
    weighted = jnp.einsum("rgqk,kgd->rgqd", probs, value_split, preferred_element_type=jnp.float32)
    result = (weighted / total[..., None]).reshape(count, head_count * HD)
    return (result, (top + jnp.log(total)).reshape(count, head_count))


def cache_block(query_rows, cache_keys, cache_values):
    count = query_rows.shape[0]
    width = math.gcd(count, 64)
    blocks = query_rows.reshape(count // width, width, query_rows.shape[1])

    def one_block(block):
        return partial_attend(block, cache_keys, cache_values, None)

    results, log_totals = lax.map(one_block, blocks)
    return (results.reshape(count, -1), log_totals.reshape(count, -1))


def combine_all(got_out, got_log, own_out, own_log):
    sources = got_out.shape[0]
    count, width = own_out.shape
    head_count = own_log.shape[1]
    top = jnp.maximum(jnp.max(got_log, axis=0), own_log)
    weights = jnp.exp(got_log - top[None])
    own_weight = jnp.exp(own_log - top)
    total = jnp.sum(weights, axis=0) + own_weight
    summed = jnp.sum(got_out.reshape(sources, count, head_count, HD) * weights[..., None], axis=0)
    summed = summed + own_out.reshape(count, head_count, HD) * own_weight[..., None]
    return (summed / total[..., None]).reshape(count, width)


def local(
    queries,
    turn_keys,
    turn_values,
    cache_keys,
    cache_values,
    positions,
    span_bounds,
    residual,
    out_weight,
):
    own_queries = queries[0]
    own_keys = turn_keys[0]
    own_values = turn_values[0]
    local_keys = cache_keys[0]
    local_values = cache_values[0]
    devices = lax.axis_size("context")
    index = lax.axis_index("context")
    tok_rows = own_queries.shape[0]
    head_count = own_queries.shape[1] // HD
    all_position = positions[0]
    own_position = lax.dynamic_slice_in_dim(all_position, index * tok_rows, tok_rows)
    allowed = span_mask(own_position, all_position, span_bounds[0])
    piece_q = lax.all_gather(own_queries, "context", axis=0, tiled=True)
    piece_k = lax.all_gather(own_keys, "context", axis=0, tiled=True)
    piece_v = lax.all_gather(own_values, "context", axis=0, tiled=True)
    part_out, part_log = cache_block(piece_q, local_keys, local_values)
    out_all = part_out
    log_all = part_log
    key_store = piece_k
    value_store = piece_v
    out_all, log_all, key_store, value_store = (out_all, log_all, key_store, value_store)
    got_out, got_log = (
        lax.all_to_all(
            out_all.reshape(devices, tok_rows, head_count * HD),
            "context",
            split_axis=0,
            concat_axis=0,
            tiled=True,
        ),
        lax.all_to_all(
            log_all.reshape(devices, tok_rows, head_count),
            "context",
            split_axis=0,
            concat_axis=0,
            tiled=True,
        ),
    )
    turn_out, turn_log = partial_attend(own_queries, key_store, value_store, allowed)
    merged = combine_all(got_out, got_log, turn_out, turn_log)
    attended = merged.astype(jnp.bfloat16)
    weight = out_weight[0]
    projected = jnp.dot(
        lax.all_gather(attended, "context", axis=0, tiled=True),
        weight,
        preferred_element_type=jnp.float32,
    )
    summed = lax.psum_scatter(projected, "tensor", scatter_dimension=0, tiled=True)
    layer_out = (residual[0].astype(jnp.float32) + summed).astype(jnp.bfloat16)
    handed = shifted(layer_out, "section", 1)
    return handed[None]


def solution(mesh):
    placed = (
        P("section", "context", "tensor"),
        P("section", "context", "tensor"),
        P("section", "context", "tensor"),
        P("section", "context", "tensor"),
        P("section", "context", "tensor"),
        P("section", None),
        P("section", None, None),
        P("section", "tensor", "context"),
        P("section", "tensor", "context"),
    )
    return jax.shard_map(
        local,
        mesh=mesh,
        in_specs=placed,
        out_specs=P("section", "tensor", "context"),
        check_vma=False,
    )
```

profile of v0, /device:TPU:1, one launch (start us, length us, event | category | flops | bytes accessed | tf_op | source)
XLA Modules:
  0.0 639.3 jit_solution(9205981556675815189)
XLA Ops:
  6.5 0.7 all-gather.8.cloned.1.call-update
  7.3 117.8 %all-gather.8.cloned.1.call-done = bf16[1,512,1024]{2,1,0:T(8,128)(2,1)} async-done(((bf16[1,16,1024]{2,1,0:T(8,128)(2,1)}), bf16[1,512,1024]{2,1,0:T(8,128)(2,1)}) %all-gather.8.cloned.1.call-update) | async-done | bytes 1048592 | tf_op jit(solution)/shard_map/all_gather | solution.py:106
  125.1 37.1 %while.12 = (s32[]{:T(128)}, f32[8,64,1024]{2,1,0:T(8,128)S(1)}, f32[8,64,8]{2,1,0:T(8,128)S(1)}, bf16[8,64,1024]{2,1,0:T(8,128)(2,1)}, bf16[1,2048,128]{2,1,0:T...) while((s32[]{:T(128)}, f32[8,64,1024]{2,1,0:T(8,128)S(1)}, f32[8,64,8]{2,1,0:T(8,128)S(1)}, ...), condition=%wide.region_3.4_spmd, body=%wide.region_0.3_spmd.sunk | while | flops 545324544 | bytes 17803388 | solution.py:66
  125.1 0.9 dynamic-slice_bitcast_fusion.3
  126.0 1.9 bitcast_reduce_fusion.3
  127.9 0.8 fusion.63
  128.7 0.8 fusion.64
  129.7 0.9 dynamic-slice_bitcast_fusion.3
  130.7 1.9 bitcast_reduce_fusion.3
  132.6 0.8 fusion.63
  133.4 0.8 fusion.64
  134.3 0.9 dynamic-slice_bitcast_fusion.3
  135.3 1.9 bitcast_reduce_fusion.3
  137.2 0.8 fusion.63
  138.0 0.8 fusion.64
  139.0 0.9 dynamic-slice_bitcast_fusion.3
  139.9 1.9 bitcast_reduce_fusion.3
  141.8 0.8 fusion.63
  142.7 0.8 fusion.64
  143.6 0.9 dynamic-slice_bitcast_fusion.3
  144.6 1.9 bitcast_reduce_fusion.3
  146.5 0.8 fusion.63
  147.3 0.8 fusion.64
  148.3 0.9 dynamic-slice_bitcast_fusion.3
  149.2 1.9 bitcast_reduce_fusion.3
  151.1 0.8 fusion.63
  151.9 0.8 fusion.64
  152.9 0.9 dynamic-slice_bitcast_fusion.3
  153.9 1.9 bitcast_reduce_fusion.3
  155.8 0.8 fusion.63
  156.6 0.8 fusion.64
  157.5 0.9 dynamic-slice_bitcast_fusion.3
  158.5 1.9 bitcast_reduce_fusion.3
  160.4 0.8 fusion.63
  161.2 0.8 fusion.64
  162.3 0.1 copy.44
  162.4 0.1 reshape.162
  162.5 21.3 %all_to_all.10 = f32[32,1,128]{2,1,0:T(1,128)S(1)} all-to-all(f32[32,1,128]{2,1,0:T(1,128)S(1)} %reshape.162), channel_id=1, replica_groups=mesh['section'=2,'context'=32,'tensor'=8] {'context'}, dimensions={0} | all-to-all | bytes 32768 | tf_op jit(solution)/shard_map/all_to_all | solution.py:123
  183.8 4.0 all-to-all-start
  187.9 114.0 %all-gather.1 = bf16[1,512,128]{2,1,0:T(8,128)(2,1)S(1)} all-gather(bf16[1,16,128]{2,1,0:T(8,128)(2,1)S(1)} %copy-done.4), channel_id=3, replica_groups=mesh['section'=2,'context'=32,'tensor'=8] {'context'}, dimensions={1}, use_global_device_ids=true | all-gather | bytes 135168 | tf_op jit(solution)/shard_map/all_gather | solution.py:107
  301.9 0.2 fusion.23
  302.1 0.3 fusion.52
  302.4 0.2 fusion.29
  302.7 46.7 %all-gather.2 = bf16[1,512,128]{2,1,0:T(8,128)(2,1)S(1)} all-gather(bf16[1,16,128]{2,1,0:T(8,128)(2,1)S(1)} %copy-done.5), channel_id=4, replica_groups=mesh['section'=2,'context'=32,'tensor'=8] {'context'}, dimensions={1}, use_global_device_ids=true | all-gather | bytes 135168 | tf_op jit(solution)/shard_map/all_gather | solution.py:108
  349.4 0.2 fusion.24
  349.6 0.5 broadcast.41
  350.1 0.7 reduce.5
  350.8 0.1 reshape.163
  350.9 0.1 copy.49
  351.1 0.2 fusion.51
  351.4 0.2 copy.50
  351.6 1.9 mul.54
  353.6 2.7 mul.55
  356.3 1.8 multiply_reduce_fusion
  358.2 0.1 div.36
  358.2 0.1 mul.57
  358.3 0.7 fusion.33
  359.1 158.7 %all-gather.6.cloned.1.call-done = bf16[512,1024]{1,0:T(8,128)(2,1)} async-done(((bf16[16,1024]{1,0:T(8,128)(2,1)}), bf16[512,1024]{1,0:T(8,128)(2,1)}) %all-gather.6.cloned.1.call-update) | async-done | bytes 1048592 | tf_op jit(solution)/shard_map/all_gather | solution.py:136
  517.8 2.5 fusion.25
  520.3 105.7 %reduce-scatter.2.cloned.1.call-done = f32[64,256]{1,0:T(8,128)} async-done(((f32[512,256]{1,0:T(8,128)}), f32[64,256]{1,0:T(8,128)}) %reduce-scatter.2.cloned.1.call-update) | async-done | bytes 65552 | tf_op jit(solution)/shard_map/reduce_scatter | solution.py:140
  626.0 0.8 fusion.35
  626.9 4.5 collective-permute-start
  631.3 0.8 collective-permute-done
  632.1 0.6 copy.89
  (83 shorter events, 1.6 us)
Async XLA Ops:
  6.5 511.3 %copy-start = (bf16[1,1024,256]{2,1,0:T(8,128)(2,1)S(1)}, bf16[1,1024,256]{2,1,0:T(8,128)(2,1)}, u32[]{:S(2)}) copy-start(bf16[1,1024,256]{2,1,0:T(8,128)(2,1)} %param.19) | copy-start | bytes 1572868
  6.5 118.5 %all-gather.8.cloned.1.call-start = ((), (), s32[]{:S(2)}) async-start(), calls=%async_computation.5 | async-start | bytes 1081344 | tf_op jit(solution)/shard_map/all_gather | solution.py:106
  126.0 2.7 copy-start.7
  130.7 2.7 copy-start.7
  135.3 2.7 copy-start.7
  139.9 2.7 copy-start.7
  144.6 2.7 copy-start.7
  149.2 2.7 copy-start.7
  153.9 2.7 copy-start.7
  158.5 2.7 copy-start.7
  162.2 21.6 %copy-start.1 = (f32[8,64,1024]{2,1,0:T(8,128)}, f32[8,64,1024]{2,1,0:T(8,128)S(1)}, u32[]{:S(2)}) copy-start(f32[8,64,1024]{2,1,0:T(8,128)S(1)} %get-tuple-element.38) | copy-start | bytes 6291460
  162.2 25.7 %copy-start.2 = (bf16[1,16,1024]{2,1,0:T(8,128)(2,1)S(1)}, bf16[1,16,1024]{2,1,0:T(8,128)(2,1)}, u32[]{:S(2)}) copy-start(bf16[1,16,1024]{2,1,0:T(8,128)(2,1)} %param.11) | copy-start | bytes 98308
  162.2 25.7 %copy-start.4 = (bf16[1,16,128]{2,1,0:T(8,128)(2,1)S(1)}, bf16[1,16,128]{2,1,0:T(8,128)(2,1)}, u32[]{:S(2)}) copy-start(bf16[1,16,128]{2,1,0:T(8,128)(2,1)} %param.12) | copy-start | bytes 12292
  162.2 139.6 %copy-start.8 = (s32[1,512]{1,0:T(1,128)S(1)}, s32[1,512]{1,0:T(1,128)}, u32[]{:S(2)}) copy-start(s32[1,512]{1,0:T(1,128)} %param.16) | copy-start | bytes 6148
  162.2 139.7 %copy-start.6 = (s32[1,4,2]{1,2,0:T(2,128)S(1)}, s32[1,4,2]{1,2,0:T(2,128)}, u32[]{:S(2)}) copy-start(s32[1,4,2]{1,2,0:T(2,128)} %param.17) | copy-start | bytes 100
  162.2 140.4 %copy-start.5 = (bf16[1,16,128]{2,1,0:T(8,128)(2,1)S(1)}, bf16[1,16,128]{2,1,0:T(8,128)(2,1)}, u32[]{:S(2)}) copy-start(bf16[1,16,128]{2,1,0:T(8,128)(2,1)} %param.13) | copy-start | bytes 12292
  183.8 172.5 %all-to-all-start = ((f32[32,16,1024]{2,1,0:T(8,128)}), f32[32,16,1024]{2,1,0:T(8,128)S(1)}, u32[]{:S(2)}, u32[]{:S(2)}) async-start(f32[32,16,1024]{2,1,0:T(8,128)} %bitcast.156), calls=%async_computation | async-start | bytes 4194304 | tf_op jit(solution)/shard_map/all_to_all | solution.py:116
  187.8 330.0 %all-gather.6.cloned.1.call-start = ((), (), s32[]{:S(2)}) async-start(), calls=%async_computation.3 | async-start | bytes 1081344 | tf_op jit(solution)/shard_map/all_gather | solution.py:136
  356.2 269.8 %copy-start.3 = (bf16[1,64,256]{2,1,0:T(8,128)(2,1)S(1)}, bf16[1,64,256]{2,1,0:T(8,128)(2,1)}, u32[]{:S(2)}) copy-start(bf16[1,64,256]{2,1,0:T(8,128)(2,1)} %param.18) | copy-start | bytes 98308
  359.0 267.0 %reduce-scatter.2.cloned.1.call-start = ((), (), s32[]{:S(2)}) async-start(), calls=%async_computation.4 | async-start | bytes 589824 | tf_op jit(solution)/shard_map/reduce_scatter | solution.py:140
  626.9 5.3 collective-permute-start
Sparse Core Ops, SparseCore 0:
  9.4 115.5 all-gather.7
  359.1 158.6 all-gather.5
  522.2 103.7 reduce-scatter.1
where the time goes:
time: 640 us; the launch traced here: 639 us
  waiting for transfers between devices  384 us (60%)
  blocking collectives  182 us (28%)
  matrix products  24.9 us (4%)
  local copies, waits for them, and re-layouts  15.1 us (2%)
  between operations  13.3 us (2%)
  other arithmetic  11.1 us (2%)
  starting transfers between devices  8.55 us (1%)
    all_gather x1, waiting for transfers between devices, local(): lax.all_gather(attended, 'context', axis=0, tiled=True)  159 us
    all_gather x1, waiting for transfers between devices, local(): piece_q = lax.all_gather(own_queries, 'context', axis=0, tiled=True)  118 us
    all_gather x1, blocking collectives, local(): piece_k = lax.all_gather(own_keys, 'context', axis=0, tiled=True)  114 us
    reduce_scatter x1, waiting for transfers between devices, local(): lax.psum_scatter(projected, 'tensor', scatter_dimension=0, tiled=True)  106 us
    all_gather x1, blocking collectives, local(): piece_v = lax.all_gather(own_values, 'context', axis=0, tiled=True)  46.7 us
    all_to_all x1, blocking collectives, local(): lax.all_to_all(log_all.reshape(devices, tok_rows, head_count), 'context',...  21.3 us
    dot_general x9, matrix products, partial_attend(): jnp.einsum('rgqd,kgd->rgqk', query_split, key_split, preferred_element_ty...  15.4 us
  transfers between devices with their start and end apart: 5, of which 4 were waited for; matrix products, arithmetic and copies ran while one was open for 1% of the time, Pallas kernels for 0%

commit v1 on v0

v1 whole, which is shorter than its diff:
```python
import functools
import math

import jax
import jax.numpy as jnp
from jax import lax
from jax.experimental import pallas as pl
from jax.experimental.pallas import tpu as pltpu
from jax.sharding import PartitionSpec as P

MESH = pl.DeviceIdType.MESH
HD = 128
NEG = -1e30
NZ = 16
KEYS = 2048
ROWS = 16
TILE = 256
BLOCK = 512
PACK = HD + 16
SCALE = math.log2(math.e) / math.sqrt(HD)
NT = (((1,), (1,)), ((), ()))
F32, BF16 = jnp.float32, jnp.bfloat16

ORDER = [
    ("A", 0), ("B", 0), ("A", 1), ("A", -1), ("A", 2), ("A", -2), ("B", 1), ("B", -1),
    ("A", 5), ("A", -5), ("A", 3), ("A", -3), ("B", 2), ("B", -2), ("A", 4), ("A", -4),
    ("B", 5), ("B", -5), ("A", 6), ("A", -6), ("A", 7), ("A", -7), ("A", 8), ("B", 3),
    ("B", -3), ("B", 4), ("B", -4), ("B", 8), ("B", 6), ("B", -6), ("B", 7), ("B", -7),
]
SLOT = {chunk: i for i, chunk in enumerate(ORDER)}
TILES = len(ORDER) // 2
XORDER = [0, 1, -1, 2, -2, 5, -5, 3, -3, 4, -4, 6, -6, 7, -7, 8]
XSLOT = {o: i for i, o in enumerate(XORDER)}
HOP = {8: 3, 7: 2, 6: 1, 5: 5, 4: 2, 3: 1, 2: 2, 1: 1}


def pack(values, total, offset):
    row = lax.broadcasted_iota(jnp.int32, (16, values.shape[1]), 0)
    total_hi = total.astype(BF16).astype(F32)
    offset_hi = offset.astype(BF16).astype(F32)
    tail = jnp.where(row == 0, total_hi, 0.0)
    tail = jnp.where(row == 1, total - total_hi, tail)
    tail = jnp.where(row == 2, offset_hi, tail)
    tail = jnp.where(row == 3, offset - offset_hi, tail)
    return values.astype(BF16), tail.astype(BF16)


def merge(blocks):
    tails = [b[HD:PACK].astype(F32) for b in blocks]
    totals = [t[0:1] + t[1:2] for t in tails]
    offsets = [t[2:3] + t[3:4] for t in tails]
    top = functools.reduce(jnp.maximum, offsets)
    factors = [jnp.exp2(o - top) for o in offsets]
    total = sum(t * f for t, f in zip(totals, factors))
    values = sum(b[:HD].astype(F32) * f for b, f in zip(blocks, factors))
    return values, total, top


def kernel(
    q_ref, tk_ref, tv_ref, k_hbm, v_hbm, pos_ref, span_ref, res_hbm, w_hbm,
    out_ref,
    qbuf, kk, vraw, vt, s0, s1, m0, m1, limit, limit_rows, key_pos, obuf, arecv, rrecv, xbuf, wbuf, proj, pbuf, res, rbuf,
    load_sem, q_recv, a_recv, r_recv, x_recv, w_recv, p_recv, res_recv, send,
):
    s = lax.axis_index("section")
    c = lax.axis_index("context")
    t = lax.axis_index("tensor")
    z, y = c // 2, lax.rem(c, 2)

    def along(distance):
        return (s, lax.rem(z + distance + 2 * NZ, NZ) * 2 + y, t)

    partner = (s, z * 2 + 1 - y, t)

    def plane(to_y, to_t):
        return (1 - s, z * 2 + to_y, to_t)

    def remote(src, dst, send_sem, recv_sem, device):
        return pltpu.make_async_remote_copy(src, dst, send_sem, recv_sem, device_id=device, device_id_type=MESH)

    barrier = pltpu.get_barrier_semaphore()
    for d in (5, 2, 1, 3):
        for sign in (1, -1):
            pl.semaphore_signal(barrier, inc=1, device_id=along(sign * d), device_id_type=MESH)
    pl.semaphore_signal(barrier, inc=1, device_id=partner, device_id_type=MESH)
    for to_y in range(2):
        for to_t in range(8):
            pl.semaphore_signal(barrier, inc=1, device_id=plane(to_y, to_t), device_id_type=MESH)

    loads = [
        pltpu.make_async_copy(v_hbm, vraw, load_sem.at[0]),
        pltpu.make_async_copy(k_hbm, kk.at[pl.ds(0, KEYS), pl.ds(0, HD)], load_sem.at[1]),
        pltpu.make_async_copy(k_hbm, kk.at[pl.ds(0, KEYS), pl.ds(HD, HD)], load_sem.at[2]),
        pltpu.make_async_copy(w_hbm, wbuf.at[y], load_sem.at[3]),
        pltpu.make_async_copy(res_hbm, res, load_sem.at[4]),
    ]
    for load in loads:
        load.start()
    for h in range(8):
        qbuf[0, pl.ds(h * ROWS, ROWS), :] = q_ref[:, h * HD : (h + 1) * HD]

    pl.semaphore_wait(barrier, 25)

    def q_send(src, dst, device, which):
        remote(qbuf.at[src], qbuf.at[dst], send.at[which], q_recv.at[dst], device).start()

    def q_wait(slot):
        remote(qbuf.at[slot], qbuf.at[slot], send.at[0], q_recv.at[slot], partner).wait_recv()

    for d in (5, 2, 1):
        for sign in (1, -1):
            q_send(0, SLOT["A", -sign * d], along(sign * d), 0)
        if d == 5:
            q_send(0, SLOT["B", 0], partner, 1)

    def arrive(d):
        for sign in (1, -1):
            src = SLOT["A", -sign * d]
            q_wait(src)
            for far, step in {5: ((7, 2), (6, 1)), 2: ((4, 2), (3, 1))}.get(d, ()):
                q_send(src, SLOT["A", -sign * far], along(sign * step), 0)
        if d == 5:
            q_send(SLOT["A", 5] + 1 - s, SLOT["A", 8], along((1 - 2 * s) * 3), 0)
        for sign in (1, -1):
            q_send(SLOT["A", -sign * d], SLOT["B", -sign * d], partner, 1)

    def arrive_last():
        q_wait(SLOT["A", 8])
        q_send(SLOT["A", 8], SLOT["B", 8], partner, 1)

    row = lax.broadcasted_iota(jnp.int32, (16, KEYS + ROWS), 0)
    vt[HD:PACK, :] = jnp.where(row == 0, 1.0, 0.0).astype(BF16)
    vt[0:HD, KEYS : KEYS + ROWS] = tv_ref[...].astype(F32).T.astype(BF16)
    kk[KEYS : KEYS + ROWS, 0:HD] = tk_ref[...]
    kk[KEYS : KEYS + ROWS, HD : 2 * HD] = tk_ref[...]
    position = pos_ref[...].astype(F32)
    seen = position + 1.0
    for j in range(4):
        start = span_ref[j, 0].astype(F32)
        end = span_ref[j, 1].astype(F32)
        inside = (start <= position) & (position < end)
        seen = jnp.where(inside, jnp.maximum(seen, end), seen)
    lane = lax.broadcasted_iota(jnp.int32, (32, 512), 1)
    chunk_row = lax.broadcasted_iota(jnp.int32, (32, 512), 0)
    spread = jnp.where(lane // ROWS == chunk_row, seen, 0.0)
    spread_hi = spread.astype(BF16)
    spread_lo = (spread - spread_hi.astype(F32)).astype(BF16)
    pick = jnp.where(
        lax.rem(lax.broadcasted_iota(jnp.int32, (512, HD), 0), ROWS)
        == lax.rem(lax.broadcasted_iota(jnp.int32, (512, HD), 1), ROWS),
        1.0,
        0.0,
    ).astype(BF16)
    limit_rows[...] = jnp.dot(spread_hi, pick, preferred_element_type=F32) + jnp.dot(
        spread_lo, pick, preferred_element_type=F32
    )
    key_lane = lax.broadcasted_iota(jnp.int32, (ROWS, 512), 1)
    key_row = lax.broadcasted_iota(jnp.int32, (ROWS, 512), 0)
    own = jnp.where(key_lane == key_row + c * ROWS, position, 0.0)
    key_pos[...] = jnp.broadcast_to(jnp.sum(own, axis=1, keepdims=True), (ROWS, HD))
    for i, (kind, o) in enumerate(ORDER):
        chunk = lax.rem(z + o + NZ, NZ) * 2 + (y if kind == "A" else 1 - y)
        limit[i // 2, :, (i % 2) * HD : (i % 2 + 1) * HD] = jnp.broadcast_to(
            limit_rows[pl.ds(chunk, 1), :], (8, HD)
        )
    loads[0].wait()
    for b in range(KEYS // HD):
        vt[0:HD, b * HD : (b + 1) * HD] = vraw[b * HD : (b + 1) * HD, :].T
    loads[1].wait()
    loads[2].wait()

    def step(scores_of, s_new, m_new, values_of, s_old, m_old):
        top = acc = offset = query = None
        if scores_of is not None:
            scaled = qbuf[pl.ds(2 * scores_of, 2)].reshape(TILE, HD).astype(F32) * SCALE
            high = scaled.astype(BF16)
            query = jnp.concatenate([high, (scaled - high.astype(F32)).astype(BF16)], axis=1)
        if values_of is not None:
            offset = jnp.ceil(jnp.max(m_old[...], axis=0, keepdims=True))
        for first in range(0, KEYS + ROWS, BLOCK):
            keys = min(BLOCK, KEYS + ROWS - first)
            if scores_of is not None:
                scores = lax.dot_general(kk[first : first + keys, :], query, NT, preferred_element_type=F32)
                if first == KEYS:
                    far = jnp.concatenate([key_pos[...], key_pos[...]], axis=1)
                    scores = jnp.where(far < limit[scores_of][0:1], scores, NEG)
                s_new[first : first + keys, :] = scores
                most = jnp.max(scores.reshape(keys // 8, 8, TILE), axis=0)
                top = most if top is None else jnp.maximum(top, most)
            if values_of is not None:
                probs = jnp.exp2(s_old[first : first + keys, :] - offset).astype(BF16)
                part = jnp.dot(vt[:, first : first + keys], probs, preferred_element_type=F32)
                acc = part if acc is None else acc + part
        if scores_of is not None:
            m_new[...] = top
        if values_of is not None:
            values, tail = pack(acc[:HD], acc[HD : HD + 1], offset)
            for half in range(2):
                obuf[2 * values_of + half, 0:HD, :] = values[:, half * HD : (half + 1) * HD]
                obuf[2 * values_of + half, HD:PACK, :] = tail[:, half * HD : (half + 1) * HD]

    before = {i: [] for i in range(TILES)}
    after = {i: [] for i in range(TILES)}
    before[0].append(lambda: q_wait(SLOT["B", 0]))
    before[1].append(lambda: arrive(1))
    before[2].append(lambda: arrive(2))
    before[3].append(lambda: arrive(5))
    before[5].append(lambda: arrive(3))
    before[6].append(lambda: arrive(4))
    before[8].append(lambda: arrive(6))
    before[9].append(lambda: arrive(7))
    before[10].append(arrive_last)
    for i, (kind, o) in enumerate(ORDER):
        if kind == "B" and o != 0:
            before[i // 2].append(functools.partial(q_wait, i))
        if kind == "A":
            after[i // 2].append(
                functools.partial(
                    lambda src, dst: remote(obuf.at[src], arecv.at[dst], send.at[2], a_recv.at[dst], partner).start(),
                    i,
                    XSLOT[o],
                )
            )

    def run(events, tile, j=None, of=None):
        if j is None:
            for event in events[tile]:
                event()
            return
        for at in range(TILES // 2 - 1):
            todo = events[2 * at + of]
            if todo:

                @pl.when(j == at)
                def _(todo=todo):
                    for event in todo:
                        event()

    run(before, 0)
    step(0, s0, m0, None, None, None)

    def two(j, carry):
        run(before, None, j, 1)
        step(2 * j + 1, s1, m1, 2 * j, s0, m0)
        run(after, None, j, 0)
        run(before, None, j, 2)
        step(2 * j + 2, s0, m0, 2 * j + 1, s1, m1)
        run(after, None, j, 1)
        return carry

    lax.fori_loop(0, TILES // 2 - 1, two, 0)
    run(before, TILES - 1)
    step(TILES - 1, s1, m1, TILES - 2, s0, m0)
    run(after, TILES - 2)
    step(None, None, None, TILES - 1, s1, m1)
    run(after, TILES - 1)

    loads[3].wait()
    remote(wbuf.at[y], wbuf.at[y], send.at[3], w_recv, partner).start()
    loads[4].wait()
    remote(res, rbuf, send.at[4], res_recv, plane(y, t)).start()

    def a_wait(slot):
        remote(obuf.at[0], arecv.at[slot], send.at[2], a_recv.at[slot], partner).wait_recv()

    def r_wait(side, d):
        remote(obuf.at[0], rrecv.at[side, d], send.at[5], r_recv.at[side, d], partner).wait_recv()

    def reduce_to(side, d, slot, aslot, parts):
        a_wait(aslot)
        for part in parts:
            r_wait(side, part)
        values, total, offset = merge([obuf[slot], arecv[aslot]] + [rrecv[side, part] for part in parts])
        values, tail = pack(values, total, offset)
        obuf[slot, 0:HD, :] = values
        obuf[slot, HD:PACK, :] = tail
        device = along((1 - 2 * side) * HOP[d])
        remote(obuf.at[slot], rrecv.at[side, d], send.at[5], r_recv.at[side, d], device).start()

    def signed(side, d):
        return d * (1 - 2 * side)

    reduce_to(s, 8, SLOT["B", 8], XSLOT[8], [])
    for d in (7, 6, 4, 3):
        for side in range(2):
            reduce_to(side, d, SLOT["B", signed(side, d)], XSLOT[signed(side, d)], [])
    for side in range(2):
        reduce_to(side, 1, SLOT["B", signed(side, 1)], XSLOT[signed(side, 1)], [])
    reduce_to(1 - s, 5, SLOT["B", 5] + 1 - s, XSLOT[5] + 1 - s, [7, 6])
    reduce_to(s, 5, SLOT["B", 5] + s, XSLOT[5] + s, [7, 6, 8])
    for side in range(2):
        reduce_to(side, 2, SLOT["B", signed(side, 2)], XSLOT[signed(side, 2)], [4, 3])
    a_wait(0)
    for d in (1, 2, 5):
        for side in range(2):
            r_wait(side, d)
    values, total, _ = merge(
        [obuf[SLOT["B", 0]], arecv[0]] + [rrecv[side, d] for d in (1, 2, 5) for side in range(2)]
    )
    xbuf[0] = (values / total).T.astype(BF16)

    def x_send(src, dst, device):
        remote(xbuf.at[src], xbuf.at[dst], send.at[6], x_recv.at[dst], device).start()

    def x_wait(slot):
        remote(xbuf.at[slot], xbuf.at[slot], send.at[6], x_recv.at[slot], partner).wait_recv()

    for d in (5, 2, 1):
        for sign in (1, -1):
            x_send(0, XSLOT[-sign * d], along(sign * d))

    def x_arrive(d):
        for sign in (1, -1):
            src = XSLOT[-sign * d]
            x_wait(src)
            for far, step_ in {5: ((7, 2), (6, 1)), 2: ((4, 2), (3, 1))}.get(d, ()):
                x_send(src, XSLOT[-sign * far], along(sign * step_))
        if d == 5:
            x_send(XSLOT[5] + 1 - s, XSLOT[8], along((1 - 2 * s) * 3))

    def project(offsets):
        rows = jnp.concatenate(
            [jnp.concatenate([xbuf[XSLOT[o], h * ROWS : (h + 1) * ROWS, :] for h in range(8)], axis=1) for o in offsets],
            axis=0,
        )
        first = XSLOT[offsets[0]] * ROWS
        for to_y in range(2):
            done = jnp.dot(rows, wbuf[to_y], preferred_element_type=F32)
            proj[to_y, first : first + ROWS * len(offsets), :] = done.astype(BF16)
        for i, o in enumerate(offsets):
            chip = lax.rem(z + o + NZ, NZ)
            place = (lax.rem(chip, 2) * 2 + 1 - y) * ROWS
            for to_y in range(2):
                remote(
                    proj.at[to_y, pl.ds(first + i * ROWS, ROWS)],
                    pbuf.at[t, pl.ds(pl.multiple_of(place, ROWS), ROWS)],
                    send.at[7],
                    p_recv,
                    plane(to_y, chip // 2),
                ).start()

    x_arrive(1)
    x_arrive(2)
    remote(wbuf.at[y], wbuf.at[1 - y], send.at[3], w_recv, partner).wait_recv()
    project([0, 1, -1, 2, -2])
    x_arrive(5)
    project([5, -5])
    x_arrive(3)
    project([3, -3])
    x_arrive(4)
    project([4, -4])
    x_arrive(6)
    project([6, -6])
    x_arrive(7)
    project([7, -7])
    x_wait(XSLOT[8])
    project([8])

    remote(res, rbuf, send.at[4], res_recv, partner).wait_recv()
    pltpu.make_async_copy(pbuf, pbuf, p_recv).wait()
    total = rbuf[...].astype(F32)
    for group in range(8):
        total = total + pbuf[group].astype(F32)
    out_ref[...] = total.astype(BF16)

    for which, ref in (
        (0, qbuf.at[pl.ds(0, 15)]), (1, qbuf.at[pl.ds(0, 16)]), (2, obuf.at[pl.ds(0, 16)]), (3, wbuf.at[0]),
        (4, res), (5, obuf.at[pl.ds(0, 15)]), (6, xbuf.at[pl.ds(0, 15)]), (7, proj),
    ):
        pltpu.make_async_copy(ref, ref, send.at[which]).wait()


def local(queries, turn_keys, turn_values, cache_keys, cache_values, positions, span_bounds, residual, out_weight):
    vmem = pl.BlockSpec(memory_space=pltpu.VMEM)
    smem = pl.BlockSpec(memory_space=pltpu.SMEM)
    hbm = pl.BlockSpec(memory_space=pl.ANY)
    dma = pltpu.SemaphoreType.DMA
    out = pl.pallas_call(
        kernel,
        name="prefill",
        out_shape=jax.ShapeDtypeStruct((64, 256), BF16),
        in_specs=[vmem, vmem, vmem, hbm, hbm, vmem, smem, hbm, hbm],
        out_specs=vmem,
        scratch_shapes=[
            pltpu.VMEM((32, HD, HD), BF16),
            pltpu.VMEM((KEYS + ROWS, 2 * HD), BF16),
            pltpu.VMEM((KEYS, HD), BF16),
            pltpu.VMEM((PACK, KEYS + ROWS), BF16),
            pltpu.VMEM((KEYS + ROWS, TILE), F32),
            pltpu.VMEM((KEYS + ROWS, TILE), F32),
            pltpu.VMEM((8, TILE), F32),
            pltpu.VMEM((8, TILE), F32),
            pltpu.VMEM((TILES, 8, TILE), F32),
            pltpu.VMEM((32, HD), F32),
            pltpu.VMEM((ROWS, HD), F32),
            pltpu.VMEM((32, PACK, HD), BF16),
            pltpu.VMEM((16, PACK, HD), BF16),
            pltpu.VMEM((2, 9, PACK, HD), BF16),
            pltpu.VMEM((16, HD, HD), BF16),
            pltpu.VMEM((2, 1024, 256), BF16),
            pltpu.VMEM((2, 256, 256), BF16),
            pltpu.VMEM((8, 64, 256), BF16),
            pltpu.VMEM((64, 256), BF16),
            pltpu.VMEM((64, 256), BF16),
            dma((5,)),
            dma((32,)),
            dma((16,)),
            dma((2, 9)),
            dma((16,)),
            dma,
            dma,
            dma,
            dma((8,)),
        ],
        compiler_params=pltpu.CompilerParams(collective_id=0, has_side_effects=True, vmem_limit_bytes=48 << 20),
        cost_estimate=pl.CostEstimate(flops=9 * 10**9, bytes_accessed=2 << 20, transcendentals=8 << 20),
    )(
        queries[0], turn_keys[0], turn_values[0], cache_keys[0], cache_values[0], positions, span_bounds[0], residual[0],
        out_weight[0],
    )
    return out[None]


def solution(mesh):
    placed = (
        P("section", "context", "tensor"),
        P("section", "context", "tensor"),
        P("section", "context", "tensor"),
        P("section", "context", "tensor"),
        P("section", "context", "tensor"),
        P("section", None),
        P("section", None, None),
        P("section", "tensor", "context"),
        P("section", "tensor", "context"),
    )
    return jax.shard_map(
        local,
        mesh=mesh,
        in_specs=placed,
        out_specs=P("section", "tensor", "context"),
        check_vma=False,
    )
```

time: 640 us -> 88.9 us (0.14)
  the two profiles are of different devices: /device:TPU:1 before, /device:TPU:5 now
where the time goes in v1:
time: 88.9 us; the launch traced here: 88.4 us
  Pallas kernels  82.4 us (93%)
  local copies, waits for them, and re-layouts  6.01 us (7%)
    pallas_call x1, Pallas kernels, local(): pl.pallas_call(kernel, name='prefill', out_shape=jax.ShapeDtypeStruct((64...  82.4 us
    unnamed x19, local copies, waits for them, and re-layouts  5.92 us

profile of v1, /device:TPU:5, one launch (start us, length us, event | category | flops | bytes accessed | tf_op | source)
XLA Modules:
  0.0 88.4 jit_solution(4534030370228679916)
XLA Ops:
  0.0 0.0 copy-start.8
  0.0 0.0 copy-start.7
  0.0 0.0 copy-start.5
  0.0 0.0 copy-start.6
  0.0 0.7 copy-done.8
  0.7 0.1 copy.10.span_ref
  0.8 0.0 copy-done.7
  0.8 0.0 copy-done.5
  0.8 0.0 copy-done.6
  0.8 0.0 copy-start
  0.8 1.0 %copy-done = bf16[1,2048,128]{2,1,0:T(8,128)(2,1)S(1)} copy-done((bf16[1,2048,128]{2,1,0:T(8,128)(2,1)S(1)}, bf16[1,2048,128]{2,1,0:T(8,128)(2,1)}, u32[]{:S(2)}) %copy-start) | copy-done | bytes 524312
  1.8 0.0 copy-start.1
  1.8 1.0 %copy-done.1 = bf16[1,2048,128]{2,1,0:T(8,128)(2,1)S(1)} copy-done((bf16[1,2048,128]{2,1,0:T(8,128)(2,1)S(1)}, bf16[1,2048,128]{2,1,0:T(8,128)(2,1)}, u32[]{:S(2)}) %copy-start.1) | copy-done | bytes 524312
  2.9 0.0 copy-start.2
  2.9 1.0 %copy-done.2 = bf16[1,1024,256]{2,1,0:T(8,128)(2,1)S(1)} copy-done((bf16[1,1024,256]{2,1,0:T(8,128)(2,1)S(1)}, bf16[1,1024,256]{2,1,0:T(8,128)(2,1)}, u32[]{:S(2)}) %copy-start.2) | copy-done | bytes 524312
  3.9 0.0 copy-start.3
  3.9 0.8 copy-done.3
  4.7 0.0 copy-start.4
  4.7 0.8 copy-done.4
  5.4 82.4 %prefill.1 = bf16[64,256]{1,0:T(8,128)(2,1)S(1)} custom-call(bf16[16,1024]{1,0:T(8,128)(2,1)S(1)} %bitcast.13, bf16[16,128]{1,0:T(8,128)(2,1)S(1)} %bitcast.15, bf16[16,128]{1,0:T(8,128)(2,1)S(1)} %bitcast.16, bf16[2048,128]{1,0:T(8,128)(2,1)S(1)} %bitcast.10, bf16[2048,128]{1,0:T(8,128)(2,1)S(1)} %bitcast.11, s32[1,512]{1,0:T(1,128)S(1)} %copy-done.7, ...), custom_call_target="tpu_custom_call" | custom-call | flops 8999999488 | bytes 2097152 | tf_op jit(solution)/shard_map/prefill/pallas_call | solution.py:378
  87.8 0.6 copy.12
Async XLA Ops:
  0.0 0.7 copy-start.8
  0.0 0.8 copy-start.7
  0.0 0.8 copy-start.5
  0.0 0.8 copy-start.6
  0.8 1.0 %copy-start = (bf16[1,2048,128]{2,1,0:T(8,128)(2,1)S(1)}, bf16[1,2048,128]{2,1,0:T(8,128)(2,1)}, u32[]{:S(2)}) copy-start(bf16[1,2048,128]{2,1,0:T(8,128)(2,1)} %param.12) | copy-start | bytes 1572868
  1.8 1.0 %copy-start.1 = (bf16[1,2048,128]{2,1,0:T(8,128)(2,1)S(1)}, bf16[1,2048,128]{2,1,0:T(8,128)(2,1)}, u32[]{:S(2)}) copy-start(bf16[1,2048,128]{2,1,0:T(8,128)(2,1)} %param.13) | copy-start | bytes 1572868
  2.9 1.0 %copy-start.2 = (bf16[1,1024,256]{2,1,0:T(8,128)(2,1)S(1)}, bf16[1,1024,256]{2,1,0:T(8,128)(2,1)}, u32[]{:S(2)}) copy-start(bf16[1,1024,256]{2,1,0:T(8,128)(2,1)} %param.17) | copy-start | bytes 1572868
  3.9 0.8 copy-start.3
  4.7 0.8 copy-start.4

commit v2 on v1

--- a/solution.py
+++ b/solution.py
@@ -22,15 +22,16 @@
 F32, BF16 = jnp.float32, jnp.bfloat16
 
 ORDER = [
-    ("A", 0), ("B", 0), ("A", 1), ("A", -1), ("A", 2), ("A", -2), ("B", 1), ("B", -1),
-    ("A", 5), ("A", -5), ("A", 3), ("A", -3), ("B", 2), ("B", -2), ("A", 4), ("A", -4),
-    ("B", 5), ("B", -5), ("A", 6), ("A", -6), ("A", 7), ("A", -7), ("A", 8), ("B", 3),
-    ("B", -3), ("B", 4), ("B", -4), ("B", 8), ("B", 6), ("B", -6), ("B", 7), ("B", -7),
+    ("A", 0), ("B", 0), ("A", 1), ("A", -1), ("A", 2), ("A", -2), ("A", 5), ("A", -5),
+    ("B", 1), ("B", -1), ("A", 3), ("A", -3), ("A", 4), ("A", -4), ("B", 2), ("B", -2),
+    ("A", 6), ("A", -6), ("A", 7), ("A", -7), ("A", 8), ("B", 3), ("B", -3), ("B", 4),
+    ("B", -4), ("B", 5), ("B", -5), ("B", 6), ("B", -6), ("B", 7), ("B", -7), ("B", 8),
 ]
 SLOT = {chunk: i for i, chunk in enumerate(ORDER)}
 TILES = len(ORDER) // 2
 XORDER = [0, 1, -1, 2, -2, 5, -5, 3, -3, 4, -4, 6, -6, 7, -7, 8]
 XSLOT = {o: i for i, o in enumerate(XORDER)}
+FORWARD = {5: ((7, 2), (6, 1)), 2: ((4, 2), (3, 1))}
 HOP = {8: 3, 7: 2, 6: 1, 5: 5, 4: 2, 3: 1, 2: 2, 1: 1}
 
 
@@ -57,9 +58,9 @@
 
 
 def kernel(
-    q_ref, tk_ref, tv_ref, k_hbm, v_hbm, pos_ref, span_ref, res_hbm, w_hbm,
+    q_hbm, tk_hbm, tv_hbm, k_hbm, v_hbm, pos_hbm, span_hbm, res_hbm, w_hbm,
     out_ref,
-    qbuf, kk, vraw, vt, s0, s1, m0, m1, limit, limit_rows, key_pos, obuf, arecv, rrecv, xbuf, wbuf, proj, pbuf, res, rbuf,
+    q_ref, tv_ref, pos_ref, span_ref, qbuf, kk, vraw, vt, s0, s1, m0, m1, limit, limit_rows, key_pos, obuf, arecv, rrecv, xbuf, wbuf, proj, pbuf, res, rbuf,
     load_sem, q_recv, a_recv, r_recv, x_recv, w_recv, p_recv, res_recv, send,
 ):
     s = lax.axis_index("section")
@@ -88,6 +89,12 @@
             pl.semaphore_signal(barrier, inc=1, device_id=plane(to_y, to_t), device_id_type=MESH)
 
     loads = [
+        pltpu.make_async_copy(q_hbm, q_ref, load_sem.at[5]),
+        pltpu.make_async_copy(pos_hbm, pos_ref, load_sem.at[6]),
+        pltpu.make_async_copy(tv_hbm, tv_ref, load_sem.at[7]),
+        pltpu.make_async_copy(span_hbm, span_ref, load_sem.at[10]),
+        pltpu.make_async_copy(tk_hbm, kk.at[pl.ds(KEYS, ROWS), pl.ds(0, HD)], load_sem.at[8]),
+        pltpu.make_async_copy(tk_hbm, kk.at[pl.ds(KEYS, ROWS), pl.ds(HD, HD)], load_sem.at[9]),
         pltpu.make_async_copy(v_hbm, vraw, load_sem.at[0]),
         pltpu.make_async_copy(k_hbm, kk.at[pl.ds(0, KEYS), pl.ds(0, HD)], load_sem.at[1]),
         pltpu.make_async_copy(k_hbm, kk.at[pl.ds(0, KEYS), pl.ds(HD, HD)], load_sem.at[2]),
@@ -96,6 +103,7 @@
     ]
     for load in loads:
         load.start()
+    loads[0].wait()
     for h in range(8):
         qbuf[0, pl.ds(h * ROWS, ROWS), :] = q_ref[:, h * HD : (h + 1) * HD]
 
@@ -113,31 +121,37 @@
         if d == 5:
             q_send(0, SLOT["B", 0], partner, 1)
 
-    def arrive(d):
-        for sign in (1, -1):
-            src = SLOT["A", -sign * d]
+    def arrive(kind, d):
+        for sign in (1, -1):
+            src = SLOT[kind, -sign * d]
             q_wait(src)
-            for far, step in {5: ((7, 2), (6, 1)), 2: ((4, 2), (3, 1))}.get(d, ()):
-                q_send(src, SLOT["A", -sign * far], along(sign * step), 0)
-        if d == 5:
+            for far, step in FORWARD.get(d, ()):
+                q_send(src, SLOT[kind, -sign * far], along(sign * step), 0)
+        if kind == "A" and d == 5:
             q_send(SLOT["A", 5] + 1 - s, SLOT["A", 8], along((1 - 2 * s) * 3), 0)
-        for sign in (1, -1):
-            q_send(SLOT["A", -sign * d], SLOT["B", -sign * d], partner, 1)
+        if kind == "A" and d in (2, 5):
+            for sign in (1, -1):
+                q_send(SLOT["A", -sign * d], SLOT["B", -sign * d], partner, 1)
+
+    def arrive_partner():
+        q_wait(SLOT["B", 0])
+        for sign in (1, -1):
+            q_send(SLOT["B", 0], SLOT["B", -sign], along(sign), 0)
 
     def arrive_last():
         q_wait(SLOT["A", 8])
         q_send(SLOT["A", 8], SLOT["B", 8], partner, 1)
 
+    for load in loads[1:6]:
+        load.wait()
     row = lax.broadcasted_iota(jnp.int32, (16, KEYS + ROWS), 0)
     vt[HD:PACK, :] = jnp.where(row == 0, 1.0, 0.0).astype(BF16)
     vt[0:HD, KEYS : KEYS + ROWS] = tv_ref[...].astype(F32).T.astype(BF16)
-    kk[KEYS : KEYS + ROWS, 0:HD] = tk_ref[...]
-    kk[KEYS : KEYS + ROWS, HD : 2 * HD] = tk_ref[...]
     position = pos_ref[...].astype(F32)
     seen = position + 1.0
     for j in range(4):
-        start = span_ref[j, 0].astype(F32)
-        end = span_ref[j, 1].astype(F32)
+        start = span_ref[0:1, j : j + 1].astype(F32)
+        end = span_ref[1:2, j : j + 1].astype(F32)
         inside = (start <= position) & (position < end)
         seen = jnp.where(inside, jnp.maximum(seen, end), seen)
     lane = lax.broadcasted_iota(jnp.int32, (32, 512), 1)
@@ -163,11 +177,11 @@
         limit[i // 2, :, (i % 2) * HD : (i % 2 + 1) * HD] = jnp.broadcast_to(
             limit_rows[pl.ds(chunk, 1), :], (8, HD)
         )
-    loads[0].wait()
+    loads[6].wait()
     for b in range(KEYS // HD):
         vt[0:HD, b * HD : (b + 1) * HD] = vraw[b * HD : (b + 1) * HD, :].T
-    loads[1].wait()
-    loads[2].wait()
+    loads[7].wait()
+    loads[8].wait()
 
     def step(scores_of, s_new, m_new, values_of, s_old, m_old):
         top = acc = offset = query = None
@@ -199,67 +213,6 @@
                 obuf[2 * values_of + half, 0:HD, :] = values[:, half * HD : (half + 1) * HD]
                 obuf[2 * values_of + half, HD:PACK, :] = tail[:, half * HD : (half + 1) * HD]
 
-    before = {i: [] for i in range(TILES)}
-    after = {i: [] for i in range(TILES)}
-    before[0].append(lambda: q_wait(SLOT["B", 0]))
-    before[1].append(lambda: arrive(1))
-    before[2].append(lambda: arrive(2))
-    before[3].append(lambda: arrive(5))
-    before[5].append(lambda: arrive(3))
-    before[6].append(lambda: arrive(4))
-    before[8].append(lambda: arrive(6))
-    before[9].append(lambda: arrive(7))
-    before[10].append(arrive_last)
-    for i, (kind, o) in enumerate(ORDER):
-        if kind == "B" and o != 0:
-            before[i // 2].append(functools.partial(q_wait, i))
-        if kind == "A":
-            after[i // 2].append(
-                functools.partial(
-                    lambda src, dst: remote(obuf.at[src], arecv.at[dst], send.at[2], a_recv.at[dst], partner).start(),
-                    i,
-                    XSLOT[o],
-                )
-            )
-
-    def run(events, tile, j=None, of=None):
-        if j is None:
-            for event in events[tile]:
-                event()
-            return
-        for at in range(TILES // 2 - 1):
-            todo = events[2 * at + of]
-            if todo:
-
-                @pl.when(j == at)
-                def _(todo=todo):
-                    for event in todo:
-                        event()
-
-    run(before, 0)
-    step(0, s0, m0, None, None, None)
-
-    def two(j, carry):
-        run(before, None, j, 1)
-        step(2 * j + 1, s1, m1, 2 * j, s0, m0)
-        run(after, None, j, 0)
-        run(before, None, j, 2)
-        step(2 * j + 2, s0, m0, 2 * j + 1, s1, m1)
-        run(after, None, j, 1)
-        return carry
-
-    lax.fori_loop(0, TILES // 2 - 1, two, 0)
-    run(before, TILES - 1)
-    step(TILES - 1, s1, m1, TILES - 2, s0, m0)
-    run(after, TILES - 2)
-    step(None, None, None, TILES - 1, s1, m1)
-    run(after, TILES - 1)
-
-    loads[3].wait()
-    remote(wbuf.at[y], wbuf.at[y], send.at[3], w_recv, partner).start()
-    loads[4].wait()
-    remote(res, rbuf, send.at[4], res_recv, plane(y, t)).start()
-
     def a_wait(slot):
         remote(obuf.at[0], arecv.at[slot], send.at[2], a_recv.at[slot], partner).wait_recv()
 
@@ -280,16 +233,85 @@
     def signed(side, d):
         return d * (1 - 2 * side)
 
-    reduce_to(s, 8, SLOT["B", 8], XSLOT[8], [])
-    for d in (7, 6, 4, 3):
+    def reduce_near(d):
         for side in range(2):
             reduce_to(side, d, SLOT["B", signed(side, d)], XSLOT[signed(side, d)], [])
+
+    before = {i: [] for i in range(TILES)}
+    after = {i: [] for i in range(TILES)}
+    waited = {("A", 0)}
+
+    def at(tile, event, *chunks):
+        before[tile].append(event)
+        waited.update(chunks)
+
+    at(0, arrive_partner, ("B", 0))
+    for tile, kind, d in (
+        (1, "A", 1), (2, "A", 2), (3, "A", 5), (4, "B", 2), (5, "A", 3), (6, "A", 4), (7, "B", 5), (8, "A", 6), (9, "A", 7),
+    ):
+        at(tile, functools.partial(arrive, kind, d), (kind, d), (kind, -d))
+    at(10, arrive_last, ("A", 8))
+    for i, (kind, o) in enumerate(ORDER):
+        if (kind, o) not in waited:
+            before[i // 2].append(functools.partial(q_wait, i))
+        if kind == "A":
+            after[i // 2].append(
+                functools.partial(
+                    lambda src, dst: remote(obuf.at[src], arecv.at[dst], send.at[2], a_recv.at[dst], partner).start(),
+                    i,
+                    XSLOT[o],
+                )
+            )
+
+    before[13].append(lambda: reduce_near(3))
+    before[14].append(lambda: reduce_near(4))
+    before[15].append(lambda: reduce_near(1))
+
+    def run(events, tile, j=None, of=None):
+        if j is None:
+            for event in events[tile]:
+                event()
+            return
+        for at in range(TILES // 2 - 1):
+            todo = events[2 * at + of]
+            if todo:
+
+                @pl.when(j == at)
+                def _(todo=todo):
+                    for event in todo:
+                        event()
+
+    run(before, 0)
+    step(0, s0, m0, None, None, None)
+
+    def two(j, carry):
+        run(before, None, j, 1)
+        step(2 * j + 1, s1, m1, 2 * j, s0, m0)
+        run(after, None, j, 0)
+        run(before, None, j, 2)
+        step(2 * j + 2, s0, m0, 2 * j + 1, s1, m1)
+        run(after, None, j, 1)
+        return carry
+
+    lax.fori_loop(0, TILES // 2 - 1, two, 0)
+    run(before, TILES - 1)
+    step(TILES - 1, s1, m1, TILES - 2, s0, m0)
+    run(after, TILES - 2)
+    step(None, None, None, TILES - 1, s1, m1)
+    run(after, TILES - 1)
+
+    loads[9].wait()
+    remote(wbuf.at[y], wbuf.at[y], send.at[3], w_recv, partner).start()
+    loads[10].wait()
+    remote(res, rbuf, send.at[4], res_recv, plane(y, t)).start()
+
+    reduce_to(s, 8, SLOT["B", 8], XSLOT[8], [])
+    for d in (7, 6):
+        reduce_near(d)
     for side in range(2):
-        reduce_to(side, 1, SLOT["B", signed(side, 1)], XSLOT[signed(side, 1)], [])
+        reduce_to(side, 2, SLOT["B", signed(side, 2)], XSLOT[signed(side, 2)], [4, 3])
     reduce_to(1 - s, 5, SLOT["B", 5] + 1 - s, XSLOT[5] + 1 - s, [7, 6])
     reduce_to(s, 5, SLOT["B", 5] + s, XSLOT[5] + s, [7, 6, 8])
-    for side in range(2):
-        reduce_to(side, 2, SLOT["B", signed(side, 2)], XSLOT[signed(side, 2)], [4, 3])
     a_wait(0)
     for d in (1, 2, 5):
         for side in range(2):
@@ -313,7 +335,7 @@
         for sign in (1, -1):
             src = XSLOT[-sign * d]
             x_wait(src)
-            for far, step_ in {5: ((7, 2), (6, 1)), 2: ((4, 2), (3, 1))}.get(d, ()):
+            for far, step_ in FORWARD.get(d, ()):
                 x_send(src, XSLOT[-sign * far], along(sign * step_))
         if d == 5:
             x_send(XSLOT[5] + 1 - s, XSLOT[8], along((1 - 2 * s) * 3))
@@ -364,7 +386,7 @@
     out_ref[...] = total.astype(BF16)
 
     for which, ref in (
-        (0, qbuf.at[pl.ds(0, 15)]), (1, qbuf.at[pl.ds(0, 16)]), (2, obuf.at[pl.ds(0, 16)]), (3, wbuf.at[0]),
+        (0, qbuf.at[pl.ds(0, 25)]), (1, qbuf.at[pl.ds(0, 6)]), (2, obuf.at[pl.ds(0, 16)]), (3, wbuf.at[0]),
         (4, res), (5, obuf.at[pl.ds(0, 15)]), (6, xbuf.at[pl.ds(0, 15)]), (7, proj),
     ):
         pltpu.make_async_copy(ref, ref, send.at[which]).wait()
@@ -372,16 +394,19 @@
 
 def local(queries, turn_keys, turn_values, cache_keys, cache_values, positions, span_bounds, residual, out_weight):
     vmem = pl.BlockSpec(memory_space=pltpu.VMEM)
-    smem = pl.BlockSpec(memory_space=pltpu.SMEM)
     hbm = pl.BlockSpec(memory_space=pl.ANY)
     dma = pltpu.SemaphoreType.DMA
     out = pl.pallas_call(
         kernel,
         name="prefill",
         out_shape=jax.ShapeDtypeStruct((64, 256), BF16),
-        in_specs=[vmem, vmem, vmem, hbm, hbm, vmem, smem, hbm, hbm],
+        in_specs=[hbm] * 9,
         out_specs=vmem,
         scratch_shapes=[
+            pltpu.VMEM((ROWS, 8 * HD), BF16),
+            pltpu.VMEM((ROWS, HD), BF16),
+            pltpu.VMEM((1, 512), jnp.int32),
+            pltpu.VMEM((2, 4), jnp.int32),
             pltpu.VMEM((32, HD, HD), BF16),
             pltpu.VMEM((KEYS + ROWS, 2 * HD), BF16),
             pltpu.VMEM((KEYS, HD), BF16),
@@ -402,7 +427,7 @@
             pltpu.VMEM((8, 64, 256), BF16),
             pltpu.VMEM((64, 256), BF16),
             pltpu.VMEM((64, 256), BF16),
-            dma((5,)),
+            dma((11,)),
             dma((32,)),
             dma((16,)),
             dma((2, 9)),
@@ -412,10 +437,10 @@
             dma,
             dma((8,)),
         ],
-        compiler_params=pltpu.CompilerParams(collective_id=0, has_side_effects=True, vmem_limit_bytes=48 << 20),
+        compiler_params=pltpu.CompilerParams(collective_id=0, has_side_effects=True, vmem_limit_bytes=60 << 20),
         cost_estimate=pl.CostEstimate(flops=9 * 10**9, bytes_accessed=2 << 20, transcendentals=8 << 20),
     )(
-        queries[0], turn_keys[0], turn_values[0], cache_keys[0], cache_values[0], positions, span_bounds[0], residual[0],
+        queries[0], turn_keys[0], turn_values[0], cache_keys[0], cache_values[0], positions, span_bounds[0].T, residual[0],
         out_weight[0],
     )
     return out[None]

time: 88.9 us -> 77.3 us (0.87)
  Pallas kernels: 82.4 us -> 75.8 us
  local copies, waits for them, and re-layouts: 6.01 us -> 1.38 us
    pallas_call x1, Pallas kernels: 82.4 us -> 75.8 us  [local(): pl.pallas_call(kernel, name='prefill', out_shape=jax.ShapeDtypeStruct((64...]
    unnamed x19 -> x1, local copies, waits for them, and re-layouts: 5.92 us -> 1.38 us
where the time goes in v2:
time: 77.3 us; the launch traced here: 77.1 us
  Pallas kernels  75.8 us (98%)
  local copies, waits for them, and re-layouts  1.38 us (2%)
    pallas_call x1, Pallas kernels, local(): pl.pallas_call(kernel, name='prefill', out_shape=jax.ShapeDtypeStruct((64...  75.8 us

profile of v2, /device:TPU:5, one launch (start us, length us, event | category | flops | bytes accessed | tf_op | source)
XLA Modules:
  0.0 77.1 jit_solution(3394395523670886090)
XLA Ops:
  0.0 75.8 %prefill.1 = bf16[64,256]{1,0:T(8,128)(2,1)} custom-call(bf16[16,1024]{1,0:T(8,128)(2,1)} %bitcast.15, bf16[16,128]{1,0:T(8,128)(2,1)} %bitcast.17, bf16[16,128]{1,0:T(8,128)(2,1)} %bitcast.18, bf16[2048,128]{1,0:T(8,128)(2,1)} %bitcast.12, bf16[2048,128]{1,0:T(8,128)(2,1)} %bitcast.13, s32[1,512]{1,0:T(1,128)} %pos_hbm.1, s32[2,4]{1,0:T(2,128)} %bitcast.19, ...), custom_call_target="tpu_custom_call" | custom-call | flops 8999999488 | bytes 2097152 | tf_op jit(solution)/shard_map/prefill/pallas_call | solution.py:399
  75.8 1.4 %copy.11 = bf16[1,64,256]{2,1,0:T(8,128)(2,1)} copy(bf16[1,64,256]{2,1,0:T(8,128)(2,1)} %bitcast.11) | data formatting | bytes 65536
